TPU v7x, 512 devices: a whole 4x8x8 slice. The times are simulated.
512 devices in a mesh: tm: 4 (over x), space: 128 (over z, y, core).
Axes of the slice: x: 4, y: 8, z: 8, core: 2. Of those that a mesh axis runs over, the one named last changes fastest.
Arguments:
- signal: bfloat16 [256, 256, 512], P('space', None, 'tm'), may hold values from -6 to 6
- source_boxes: int32 [256, 12], replicated, may hold values from 0 to 255
- near_boxes: int32 [256, 8], replicated, may hold values from 0 to 255, as said below
- trans_kernel: float32 [12, 256, 128], P(None, 'space'), may hold values from -0.15625 to 0.15625
- near_kernel: float32 [8, 128], replicated, may hold values from -0.1875 to 0.1875
Outputs:
- field: bfloat16 [256, 256, 512], P('space', None, 'tm')
Inputs may be any that keep to these rules, and one draw needn't show every extreme that they name: Each near_boxes[b, j] lies within 2 of b.
All inputs are finite; a program needn't handle non-finite values.
Results may differ from a plain program's by a relative error of at most 0.008.
Values may be sent and summed in bfloat16 or wider, within the bound.
No kernel may reach another device: no remote copies, remote signals or barrier semaphores. Data moves between devices by JAX's collectives and lax.ppermute only.
A program may use at most 64 MiB of HBM per device.

v0:
```python
import functools

import jax
import jax.numpy as jnp
from jax import lax
from jax.experimental import pallas as pl
from jax.experimental.pallas import tpu as pltpu
from jax.sharding import PartitionSpec as P

VMEM = pl.BlockSpec(memory_space=pltpu.VMEM)


def circulant_halves(lags, dtype):
    width = lags.shape[-1]
    rows = jnp.broadcast_to(lags, (width, width))
    turned = pltpu.roll(rows, 0, 1, stride=1, stride_axis=0)
    s = lax.broadcasted_iota(jnp.int32, (width, width), 0)
    t = lax.broadcasted_iota(jnp.int32, (width, width), 1)
    before = jnp.where(t < s, turned, 0.0).astype(dtype)
    within = jnp.where(t >= s, turned, 0.0).astype(dtype)
    return before, within


def build_kernel(source_ref, near_ref, trans_ref, slot_ref, far_ref, near_mats_ref, pick_ref):
    offsets, rays, width = trans_ref.shape
    slots = slot_ref.shape[0]
    boxes = source_ref.shape[1]
    for r in range(rays):
        for k in range(offsets):
            before, within = circulant_halves(trans_ref[k, r : r + 1, :], jnp.bfloat16)
            far_ref[r, 0:width, k * width : (k + 1) * width] = before
            far_ref[r, width : 2 * width, k * width : (k + 1) * width] = within
    for j in range(slots):
        before, within = circulant_halves(slot_ref[j : j + 1, :], jnp.bfloat16)
        near_mats_ref[0:width, j * width : (j + 1) * width] = before
        near_mats_ref[width : 2 * width, j * width : (j + 1) * width] = within
    lane = lax.broadcasted_iota(jnp.int32, (boxes, boxes), 1)
    source = jnp.transpose(source_ref[...])
    near = jnp.transpose(near_ref[...])
    for k in range(offsets + slots):
        column = source[:, k : k + 1] if k < offsets else near[:, k - offsets : k - offsets + 1]
        hit = jnp.where(column == lane, 1.0, 0.0)
        pick_ref[:, k * boxes : (k + 1) * boxes] = hit.astype(jnp.bfloat16)


def field_kernel(cur_ref, prev_ref, far_ref, near_mats_ref, pick_ref, out_ref, wide, pair, mixed):
    rays, depth, far_cols = far_ref.shape
    width = depth // 2
    boxes = pick_ref.shape[0]
    offsets, slots = far_cols // width, near_mats_ref.shape[1] // width
    for half, ref in enumerate((prev_ref, cur_ref)):
        wide[...] = ref[...].astype(jnp.float32)
        for r in range(rays):
            rows = wide[pl.ds(r, boxes, stride=rays), :]
            pair[r, :, half * width : (half + 1) * width] = rows.astype(jnp.bfloat16)
    for r in range(rays):
        own = pair[r]
        lanes = slice(r * width, (r + 1) * width)
        for k in range(0, offsets + slots, 2):
            if k < offsets:
                mats = far_ref[r, :, k * width : (k + 2) * width]
            else:
                mats = near_mats_ref[:, (k - offsets) * width : (k - offsets + 2) * width]
            two = jnp.dot(own, mats, preferred_element_type=jnp.float32).astype(jnp.bfloat16)
            mixed[k * boxes : (k + 1) * boxes, lanes] = two[:, :width]
            mixed[(k + 1) * boxes : (k + 2) * boxes, lanes] = two[:, width:]
    cut = offsets * boxes
    far = jnp.dot(pick_ref[:, :cut], mixed[:cut, :], preferred_element_type=jnp.float32)
    near = jnp.dot(pick_ref[:, cut:], mixed[cut:, :], preferred_element_type=jnp.float32)
    far = far.astype(jnp.bfloat16).astype(jnp.float32)
    near = near.astype(jnp.bfloat16).astype(jnp.float32)
    both = far + near
    for r in range(rays):
        wide[pl.ds(r, boxes, stride=rays), :] = both[:, r * width : (r + 1) * width]
    out_ref[...] = wide[...].astype(jnp.bfloat16)


def body(signal, source_boxes, near_boxes, trans_kernel, near_kernel):
    box_dev, all_rays, width = signal.shape
    devs = lax.axis_size("space")
    rays = all_rays // devs
    boxes = box_dev * devs
    offsets, slots = trans_kernel.shape[0], near_kernel.shape[0]
    mid = box_dev * rays

    parted = signal.reshape(box_dev, devs, rays, width).transpose(1, 0, 2, 3).reshape(devs, mid, width)
    current = lax.all_to_all(parted, "space", split_axis=0, concat_axis=0, tiled=True)
    size = lax.axis_size("tm")
    earlier = lax.ppermute(current, "tm", [(i, i + 1) for i in range(size - 1)])

    far_mats, near_mats, picks = pl.pallas_call(
        build_kernel,
        out_shape=(
            jax.ShapeDtypeStruct((rays, 2 * width, offsets * width), jnp.bfloat16),
            jax.ShapeDtypeStruct((2 * width, slots * width), jnp.bfloat16),
            jax.ShapeDtypeStruct((boxes, (offsets + slots) * boxes), jnp.bfloat16),
        ),
        in_specs=[VMEM] * 4,
        out_specs=(VMEM,) * 3,
        compiler_params=pltpu.CompilerParams(vmem_limit_bytes=24 << 20),
        cost_estimate=pl.CostEstimate(flops=4_000_000, bytes_accessed=8_000_000, transcendentals=0),
        name="build",
    )(
        source_boxes.T,
        near_boxes.T,
        trans_kernel.astype(jnp.bfloat16).astype(jnp.float32),
        near_kernel.astype(jnp.bfloat16).astype(jnp.float32),
    )
    field = pl.pallas_call(
        field_kernel,
        out_shape=jax.ShapeDtypeStruct((devs * mid, width), jnp.bfloat16),
        in_specs=[VMEM] * 5,
        out_specs=VMEM,
        scratch_shapes=[
            pltpu.VMEM((devs * mid, width), jnp.float32),
            pltpu.VMEM((rays, boxes, 2 * width), jnp.bfloat16),
            pltpu.VMEM(((offsets + slots) * boxes, rays * width), jnp.bfloat16),
        ],
        compiler_params=pltpu.CompilerParams(vmem_limit_bytes=24 << 20),
        cost_estimate=pl.CostEstimate(flops=1_400_000_000, bytes_accessed=6_000_000, transcendentals=0),
        name="field",
    )(
        current.reshape(devs * mid, width),
        earlier.reshape(devs * mid, width),
        far_mats,
        near_mats,
        picks,
    )
    back = lax.all_to_all(field.reshape(devs, mid, width), "space", split_axis=0, concat_axis=0, tiled=True)
    back = back.reshape(devs, box_dev, rays, width).transpose(1, 0, 2, 3)
    return back.reshape(box_dev, all_rays, width)


def solution(mesh):
    in_specs = (P("space", None, "tm"), P(), P(), P(None, "space", None), P())
    out_specs = P("space", None, "tm")
    return jax.shard_map(body, mesh=mesh, in_specs=in_specs, out_specs=out_specs, check_vma=False)
```

profile of v0, /device:TPU:1, one launch (start us, length us, event | category | flops | bytes accessed | tf_op | source)
XLA Modules:
  0.0 59.7 jit_solution(2496992602843051024)
XLA Ops:
  0.0 1.6 %copy.6 = bf16[128,2,2,128]{3,2,1,0:T(2,128)(2,1)} copy(bf16[128,2,2,128]{3,2,0,1:T(2,128)(2,1)} %bitcast.19) | data formatting | bytes 262144 | tf_op jit(solution)/shard_map/transpose | solution.py:86
  1.7 18.4 %all-to-all-start = ((bf16[128,4,128]{2,1,0:T(4,128)(2,1)}), bf16[128,4,128]{2,1,0:T(4,128)(2,1)S(1)}, u32[]{:S(2)}, u32[]{:S(2)}) async-start(bf16[128,4,128]{2,1,0:T(4,128)(2,1)} %bitcast.2), calls=%async_computation | async-start | bytes 262144 | tf_op jit(solution)/shard_map/all_to_all | solution.py:87
  20.1 0.7 %convert_convert_fusion.trans_ref = f32[12,2,128]{2,1,0:T(2,128)S(1)} fusion(f32[12,2,128]{2,1,0:T(2,128)} %param.8), kind=kLoop, calls=%fused_computation | loop fusion | flops 6144 | bytes 24576 | tf_op jit(solution)/shard_map/convert_element_type | solution.py:106
  20.8 12.0 %all-to-all-done = bf16[128,4,128]{2,1,0:T(4,128)(2,1)S(1)} async-done(((bf16[128,4,128]{2,1,0:T(4,128)(2,1)}), bf16[128,4,128]{2,1,0:T(4,128)(2,1)S(1)}, u32[]{:S(2)}, u32[]{:S(2)}) %all-to-all-start) | async-done | bytes 131104 | tf_op jit(solution)/shard_map/all_to_all | solution.py:87
  32.8 3.1 %collective-permute-start = (bf16[128,4,128]{2,1,0:T(4,128)(2,1)S(1)}, bf16[128,4,128]{2,1,0:T(4,128)(2,1)S(1)}, u32[]{:S(2)}, u32[]{:S(2)}) collective-permute-start(bf16[128,4,128]{2,1,0:T(4,128)(2,1)S(1)} %all-to-all-done), channel_id=1, source_target_pairs={{0,128},{128,256},{256,384},{1,129},{129,257},{257,385},{2,130},{1... | collective-permute-start | bytes 393224 | tf_op jit(solution)/shard_map/ppermute | solution.py:89
  35.9 0.7 %convert_convert_fusion.1.slot_ref = f32[8,128]{1,0:T(8,128)S(1)} fusion(f32[8,128]{1,0:T(8,128)} %param.9), kind=kLoop, calls=%fused_computation.1 | loop fusion | flops 2048 | bytes 8192 | tf_op jit(solution)/shard_map/convert_element_type | solution.py:107
  36.6 0.0 copy-start
  36.6 0.7 %copy-done = s32[256,12]{0,1:T(8,128)S(1)} copy-done((s32[256,12]{0,1:T(8,128)S(1)}, s32[256,12]{0,1:T(8,128)}, u32[]{:S(2)}) %copy-start) | copy-done | bytes 12312
  37.3 0.0 copy-start.1
  37.3 0.7 %copy-done.1 = s32[256,8]{0,1:T(8,128)S(1)} copy-done((s32[256,8]{0,1:T(8,128)S(1)}, s32[256,8]{0,1:T(8,128)}, u32[]{:S(2)}) %copy-start.1) | copy-done | bytes 8216
  38.0 1.2 %build.1 = (bf16[2,256,1536]{2,1,0:T(8,128)(2,1)S(1)}, bf16[256,1024]{1,0:T(8,128)(2,1)S(1)}, bf16[256,5120]{1,0:T(8,128)(2,1)S(1)}) custom-call(s32[12,256]{1,0:T(8,128)S(1)} %bitcast.15, s32[8,256]{1,0:T(8,128)S(1)} %bitcast.16, f32[12,2,128]{2,1,0:T(2,128)S(1)} %convert_convert_fusion.trans_ref, f32[8,128]{1,0:T(8,128)S(1)} %convert_convert_fusion.1.slot_ref), custom_call_target="tpu_custom_call" | custom-call | flops 4000000 | bytes 8000000 | tf_op jit(solution)/shard_map/build/pallas_call | solution.py:91
  39.3 0.0 collective-permute-done
  39.3 1.6 %field.1 = bf16[512,128]{1,0:T(8,128)(2,1)S(1)} custom-call(bf16[512,128]{1,0:T(8,128)(2,1)S(1)} %bitcast.13, bf16[512,128]{1,0:T(8,128)(2,1)S(1)} %bitcast.17, bf16[2,256,1536]{2,1,0:T(8,128)(2,1)S(1)} %get-tuple-element.8.far_ref, bf16[256,1024]{1,0:T(8,128)(2,1)S(1)} %get-tuple-element.9.near_mats_ref, bf16[256,5120]{1,0:T(8,128)(2,1)S(1)} %get-tuple-element.10.pick_ref), custom_call_target="tpu_custom_call" | custom-call | flops 1400000000 | bytes 6000000 | tf_op jit(solution)/shard_map/field/pallas_call | solution.py:109
  40.9 18.0 %all_to_all.10 = bf16[128,4,128]{2,1,0:T(4,128)(2,1)S(1)} all-to-all(bf16[128,4,128]{2,1,0:T(4,128)(2,1)S(1)} %bitcast.14), channel_id=1, replica_groups=mesh['tm'=4,'space'=128] {'space'}, dimensions={0} | all-to-all | bytes 262144 | tf_op jit(solution)/shard_map/all_to_all | solution.py:129
  58.9 0.7 %copy.7 = bf16[128,2,2,128]{3,2,0,1:T(2,128)(2,1)} copy(bf16[128,2,2,128]{3,2,1,0:T(2,128)(2,1)S(1)} %bitcast.18) | data formatting | bytes 262144 | tf_op jit(solution)/shard_map/reshape | solution.py:130
Async XLA Ops:
  1.7 31.2 %all-to-all-start = ((bf16[128,4,128]{2,1,0:T(4,128)(2,1)}), bf16[128,4,128]{2,1,0:T(4,128)(2,1)S(1)}, u32[]{:S(2)}, u32[]{:S(2)}) async-start(bf16[128,4,128]{2,1,0:T(4,128)(2,1)} %bitcast.2), calls=%async_computation | async-start | bytes 262144 | tf_op jit(solution)/shard_map/all_to_all | solution.py:87
  32.8 6.5 %collective-permute-start = (bf16[128,4,128]{2,1,0:T(4,128)(2,1)S(1)}, bf16[128,4,128]{2,1,0:T(4,128)(2,1)S(1)}, u32[]{:S(2)}, u32[]{:S(2)}) collective-permute-start(bf16[128,4,128]{2,1,0:T(4,128)(2,1)S(1)} %all-to-all-done), channel_id=1, source_target_pairs={{0,128},{128,256},{256,384},{1,129},{129,257},{257,385},{2,130},{1... | collective-permute-start | bytes 393224 | tf_op jit(solution)/shard_map/ppermute | solution.py:89
  36.6 0.7 %copy-start = (s32[256,12]{0,1:T(8,128)S(1)}, s32[256,12]{0,1:T(8,128)}, u32[]{:S(2)}) copy-start(s32[256,12]{0,1:T(8,128)} %param.6) | copy-start | bytes 36868
  37.3 0.7 %copy-start.1 = (s32[256,8]{0,1:T(8,128)S(1)}, s32[256,8]{0,1:T(8,128)}, u32[]{:S(2)}) copy-start(s32[256,8]{0,1:T(8,128)} %param.7) | copy-start | bytes 24580
where the time goes:
time: 60.2 us; the launch traced here: 59.7 us
  starting transfers between devices  21.5 us (36%)
  blocking collectives  18 us (30%)
  waiting for transfers between devices  12 us (20%)
  local copies, waits for them, and re-layouts  3.81 us (6%)
  Pallas kernels  2.85 us (5%)
  other arithmetic  1.4 us (2%)
    all_to_all x1, starting transfers between devices, body(): lax.all_to_all(parted, 'space', split_axis=0, concat_axis=0, tiled=True)  18.4 us
    all_to_all x1, blocking collectives, body(): lax.all_to_all(field.reshape(devs, mid, width), 'space', split_axis=0, co...  18 us
    all_to_all x1, waiting for transfers between devices, body(): lax.all_to_all(parted, 'space', split_axis=0, concat_axis=0, tiled=True)  12 us
    ppermute x1, starting transfers between devices, body(): earlier = lax.ppermute(current, 'tm', [(i, i + 1) for i in range(size - 1)])  3.11 us
    transpose x1, local copies, waits for them, and re-layouts, body(): signal.reshape(box_dev, devs, rays, width).transpose(1, 0, 2, 3)  1.65 us
    pallas_call x1, Pallas kernels, body(): pl.pallas_call(field_kernel, out_shape=jax.ShapeDtypeStruct((devs * mid,...  1.61 us
    unnamed x4, local copies, waits for them, and re-layouts  1.41 us
    pallas_call x1, Pallas kernels, body(): pl.pallas_call(build_kernel, out_shape=(jax.ShapeDtypeStruct((rays, 2 * w...  1.24 us
  transfers between devices with their start and end apart: 2, of which 1 were waited for; matrix products, arithmetic and copies ran while one was open for 2% of the time, Pallas kernels for 2%

commit v1 on v0

--- a/solution.py
+++ b/solution.py
@@ -8,11 +8,51 @@
 from jax.sharding import PartitionSpec as P
 
 VMEM = pl.BlockSpec(memory_space=pltpu.VMEM)
+ANY = pl.BlockSpec(memory_space=pl.ANY)
+Z, Y, CORES = 8, 8, 2
+BATCH = Y // 2 * CORES
+
+
+def ranks():
+    return [((z + Z // 2) % Z * Y + (y + Y // 2) % Y) * CORES + c for z in range(Z) for y in range(Y) for c in range(CORES)]
+
+
+def exchange(chunks):
+    return lax.all_to_all(chunks, "space", split_axis=0, concat_axis=0, axis_index_groups=[ranks()], tiled=True)
+
+
+def turned(box, z_half, y_half):
+    half = Z // 2
+    own = (box, pl.ds(z_half * half, half), y_half)
+    there = (pl.ds((1 - z_half) * half, half), 1 - y_half, slice(None), box)
+    return own, there
+
+
+def parts_kernel(signal_ref, parts_ref, sems):
+    copies = []
+    for n in range(signal_ref.shape[0] * 4):
+        own, there = turned(n // 4, n // 2 % 2, n % 2)
+        copies.append(pltpu.make_async_copy(signal_ref.at[own], parts_ref.at[there], sems.at[n]))
+    for copy in copies:
+        copy.start()
+    for copy in copies:
+        copy.wait()
+
+
+def whole_kernel(parts_ref, field_ref, sems):
+    copies = []
+    for n in range(field_ref.shape[0] * 4):
+        own, there = turned(n // 4, n // 2 % 2, n % 2)
+        copies.append(pltpu.make_async_copy(parts_ref.at[there], field_ref.at[own], sems.at[n]))
+    for copy in copies:
+        copy.start()
+    for copy in copies:
+        copy.wait()
 
 
 def circulant_halves(lags, dtype):
     width = lags.shape[-1]
-    rows = jnp.broadcast_to(lags, (width, width))
+    rows = jnp.broadcast_to(lags.astype(dtype).astype(jnp.float32), (width, width))
     turned = pltpu.roll(rows, 0, 1, stride=1, stride_axis=0)
     s = lax.broadcasted_iota(jnp.int32, (width, width), 0)
     t = lax.broadcasted_iota(jnp.int32, (width, width), 1)
@@ -21,7 +61,7 @@
     return before, within
 
 
-def build_kernel(source_ref, near_ref, trans_ref, slot_ref, far_ref, near_mats_ref, pick_ref):
+def build_kernel(source_ref, near_ref, trans_ref, slot_ref, _, far_ref, near_mats_ref, pick_ref):
     offsets, rays, width = trans_ref.shape
     slots = slot_ref.shape[0]
     boxes = source_ref.shape[1]
@@ -34,9 +74,16 @@
         before, within = circulant_halves(slot_ref[j : j + 1, :], jnp.bfloat16)
         near_mats_ref[0:width, j * width : (j + 1) * width] = before
         near_mats_ref[width : 2 * width, j * width : (j + 1) * width] = within
-    lane = lax.broadcasted_iota(jnp.int32, (boxes, boxes), 1)
-    source = jnp.transpose(source_ref[...])
-    near = jnp.transpose(near_ref[...])
+    per_dev = boxes // (Z * Y * CORES)
+    y_turn, z_turn = BATCH * per_dev, boxes // 2
+    lane = lax.broadcasted_iota(jnp.int32, (boxes, boxes), 1) ^ (y_turn | z_turn)
+
+    def by_rank(columns):
+        runs = [(p ^ (y_turn | z_turn)) for p in range(0, boxes, y_turn)]
+        return jnp.concatenate([columns[p : p + y_turn] for p in runs], axis=0)
+
+    source = by_rank(jnp.transpose(source_ref[...]))
+    near = by_rank(jnp.transpose(near_ref[...]))
     for k in range(offsets + slots):
         column = source[:, k : k + 1] if k < offsets else near[:, k - offsets : k - offsets + 1]
         hit = jnp.where(column == lane, 1.0, 0.0)
@@ -83,8 +130,17 @@
     offsets, slots = trans_kernel.shape[0], near_kernel.shape[0]
     mid = box_dev * rays
 
-    parted = signal.reshape(box_dev, devs, rays, width).transpose(1, 0, 2, 3).reshape(devs, mid, width)
-    current = lax.all_to_all(parted, "space", split_axis=0, concat_axis=0, tiled=True)
+    split = (box_dev, Z, 2, BATCH, rays, width)
+    parted = pl.pallas_call(
+        parts_kernel,
+        out_shape=jax.ShapeDtypeStruct((Z, 2, BATCH, box_dev, rays, width), signal.dtype),
+        in_specs=[ANY],
+        out_specs=VMEM,
+        scratch_shapes=[pltpu.SemaphoreType.DMA((4 * box_dev,))],
+        compiler_params=pltpu.CompilerParams(vmem_limit_bytes=4 << 20),
+        name="parts",
+    )(signal.reshape(split))
+    current = exchange(parted.reshape(devs, mid, width))
     size = lax.axis_size("tm")
     earlier = lax.ppermute(current, "tm", [(i, i + 1) for i in range(size - 1)])
 
@@ -95,7 +151,7 @@
             jax.ShapeDtypeStruct((2 * width, slots * width), jnp.bfloat16),
             jax.ShapeDtypeStruct((boxes, (offsets + slots) * boxes), jnp.bfloat16),
         ),
-        in_specs=[VMEM] * 4,
+        in_specs=[VMEM] * 4 + [ANY],
         out_specs=(VMEM,) * 3,
         compiler_params=pltpu.CompilerParams(vmem_limit_bytes=24 << 20),
         cost_estimate=pl.CostEstimate(flops=4_000_000, bytes_accessed=8_000_000, transcendentals=0),
@@ -103,8 +159,9 @@
     )(
         source_boxes.T,
         near_boxes.T,
-        trans_kernel.astype(jnp.bfloat16).astype(jnp.float32),
-        near_kernel.astype(jnp.bfloat16).astype(jnp.float32),
+        trans_kernel,
+        near_kernel,
+        current,
     )
     field = pl.pallas_call(
         field_kernel,
@@ -126,9 +183,17 @@
         near_mats,
         picks,
     )
-    back = lax.all_to_all(field.reshape(devs, mid, width), "space", split_axis=0, concat_axis=0, tiled=True)
-    back = back.reshape(devs, box_dev, rays, width).transpose(1, 0, 2, 3)
-    return back.reshape(box_dev, all_rays, width)
+    back = exchange(field.reshape(devs, mid, width))
+    whole = pl.pallas_call(
+        whole_kernel,
+        out_shape=jax.ShapeDtypeStruct(split, signal.dtype),
+        in_specs=[VMEM],
+        out_specs=ANY,
+        scratch_shapes=[pltpu.SemaphoreType.DMA((4 * box_dev,))],
+        compiler_params=pltpu.CompilerParams(vmem_limit_bytes=4 << 20),
+        name="whole",
+    )(back.reshape(Z, 2, BATCH, box_dev, rays, width))
+    return whole.reshape(signal.shape)
 
 
 def solution(mesh):

time: 60.2 us -> 54.8 us (0.910)
  blocking collectives: 18 us -> 43.7 us
  starting transfers between devices: 21.5 us -> 3.11 us
  waiting for transfers between devices: 12 us -> 0.01 us
  other arithmetic: 1.4 us -> 0 us
  Pallas kernels: 2.85 us -> 3.74 us
    all_to_all x1 -> x2, blocking collectives: 18 us -> 43.7 us  [exchange(): lax.all_to_all(chunks, 'space', split_axis=0, concat_axis=0, axis_index_g...]
    all_to_all x1 -> x0, starting transfers between devices: 18.4 us -> none  [body(): lax.all_to_all(parted, 'space', split_axis=0, concat_axis=0, tiled=True)]
    all_to_all x1 -> x0, waiting for transfers between devices: 12 us -> none  [body(): lax.all_to_all(parted, 'space', split_axis=0, concat_axis=0, tiled=True)]
    unnamed x4 -> x10, local copies, waits for them, and re-layouts: 1.41 us -> 3.71 us
    transpose x1 -> x0, local copies, waits for them, and re-layouts: 1.65 us -> none  [body(): signal.reshape(box_dev, devs, rays, width).transpose(1, 0, 2, 3)]
    convert_element_type x2 -> x0, other arithmetic: 1.4 us -> none  [the longest x1 0.71 us: body(): trans_kernel.astype(jnp.bfloat16).astype(jnp.float32)]
    pallas_call x0 -> x2, Pallas kernels: none -> 0.89 us  [the longest x1 0.71 us: body(): pl.pallas_call(whole_kernel, out_shape=jax.ShapeDtypeStruct(split, signal...]
    reshape x1 -> x0, local copies, waits for them, and re-layouts: 0.75 us -> none  [body(): back = back.reshape(devs, box_dev, rays, width).transpose(1, 0, 2, 3)]
  transfers between devices with their start and end apart: 2 -> 1, of which waited for: 1 -> 0; matrix products, arithmetic and copies ran while one was open for 2% -> 0% of each run, Pallas kernels for 2% -> 2%
where the time goes in v1:
time: 54.8 us; the launch traced here: 54.3 us
  blocking collectives  43.7 us (80%)
  Pallas kernels  3.74 us (7%)
  local copies, waits for them, and re-layouts  3.71 us (7%)
  starting transfers between devices  3.11 us (6%)
    all_to_all x2, blocking collectives, exchange(): lax.all_to_all(chunks, 'space', split_axis=0, concat_axis=0, axis_index_g...  43.7 us
    unnamed x10, local copies, waits for them, and re-layouts  3.71 us
    ppermute x1, starting transfers between devices, body(): earlier = lax.ppermute(current, 'tm', [(i, i + 1) for i in range(size - 1)])  3.11 us
    pallas_call x1, Pallas kernels, body(): pl.pallas_call(field_kernel, out_shape=jax.ShapeDtypeStruct((devs * mid,...  1.6 us
    pallas_call x1, Pallas kernels, body(): pl.pallas_call(build_kernel, out_shape=(jax.ShapeDtypeStruct((rays, 2 * w...  1.25 us
  transfers between devices with their start and end apart: 1, of which 0 were waited for; matrix products, arithmetic and copies ran while one was open for 0% of the time, Pallas kernels for 2%

profile of v1, /device:TPU:1, one launch (start us, length us, event | category | flops | bytes accessed | tf_op | source)
XLA Modules:
  0.0 54.3 jit_solution(4801852004303204056)
XLA Ops:
  0.0 0.0 copy-start
  0.0 0.9 %copy-done = bf16[2,256,128]{2,1,0:T(8,128)(2,1)S(1)} copy-done((bf16[2,256,128]{2,1,0:T(8,128)(2,1)S(1)}, bf16[2,256,128]{2,1,0:T(8,128)(2,1)}, u32[]{:S(2)}) %copy-start) | copy-done | bytes 131096
  0.9 0.2 parts.1
  1.1 25.7 %all_to_all.10._ = bf16[128,4,128]{2,1,0:T(4,128)(2,1)S(1)} all-to-all(bf16[128,4,128]{2,1,0:T(4,128)(2,1)S(1)} %bitcast.11), channel_id=1, replica_groups={{72,73,74,75,76,77,78,79,64,65,66,67,68,69,70,71,88,89,90,91,92,93,94,9..., dimensions={0} | all-to-all | bytes 262144 | tf_op jit(solution)/shard_map/all_to_all | solution.py:21
  26.8 3.1 %collective-permute-start = (bf16[128,4,128]{2,1,0:T(4,128)(2,1)S(1)}, bf16[128,4,128]{2,1,0:T(4,128)(2,1)S(1)}, u32[]{:S(2)}, u32[]{:S(2)}) collective-permute-start(bf16[128,4,128]{2,1,0:T(4,128)(2,1)S(1)} %all_to_all.10._), channel_id=1, source_target_pairs={{0,128},{128,256},{256,384},{1,129},{129,257},{257,385},{2,130},{1... | collective-permute-start | bytes 393224 | tf_op jit(solution)/shard_map/ppermute | solution.py:145
  29.9 0.0 copy-start.1
  29.9 0.7 %copy-done.1 = s32[256,12]{0,1:T(8,128)S(1)} copy-done((s32[256,12]{0,1:T(8,128)S(1)}, s32[256,12]{0,1:T(8,128)}, u32[]{:S(2)}) %copy-start.1) | copy-done | bytes 12312
  30.6 0.0 copy-start.2
  30.6 0.7 %copy-done.2 = f32[12,2,128]{2,1,0:T(2,128)S(1)} copy-done((f32[12,2,128]{2,1,0:T(2,128)S(1)}, f32[12,2,128]{2,1,0:T(2,128)}, u32[]{:S(2)}) %copy-start.2) | copy-done | bytes 12312
  31.3 0.0 copy-start.3
  31.3 0.7 %copy-done.3 = s32[256,8]{0,1:T(8,128)S(1)} copy-done((s32[256,8]{0,1:T(8,128)S(1)}, s32[256,8]{0,1:T(8,128)}, u32[]{:S(2)}) %copy-start.3) | copy-done | bytes 8216
  32.0 0.0 copy-start.4
  32.0 0.7 %copy-done.4 = f32[8,128]{1,0:T(8,128)S(1)} copy-done((f32[8,128]{1,0:T(8,128)S(1)}, f32[8,128]{1,0:T(8,128)}, u32[]{:S(2)}) %copy-start.4) | copy-done | bytes 4120
  32.7 1.2 %build.1 = (bf16[2,256,1536]{2,1,0:T(8,128)(2,1)S(1)}, bf16[256,1024]{1,0:T(8,128)(2,1)S(1)}, bf16[256,5120]{1,0:T(8,128)(2,1)S(1)}) custom-call(s32[12,256]{1,0:T(8,128)S(1)} %bitcast.14, s32[8,256]{1,0:T(8,128)S(1)} %bitcast.15, f32[12,2,128]{2,1,0:T(2,128)S(1)} %copy-done.2, f32[8,128]{1,0:T(8,128)S(1)} %copy-done.4, bf16[128,4,128]{2,1,0:T(4,128)(2,1)S(1)} %all_to_all.10._), custom_call_target="tpu_custom_call" | custom-call | flops 4000000 | bytes 8000000 | tf_op jit(solution)/shard_map/build/pallas_call | solution.py:147
  33.9 0.0 collective-permute-done
  34.0 1.6 %field.1 = bf16[512,128]{1,0:T(8,128)(2,1)S(1)} custom-call(bf16[512,128]{1,0:T(8,128)(2,1)S(1)} %bitcast.9, bf16[512,128]{1,0:T(8,128)(2,1)S(1)} %bitcast.16, bf16[2,256,1536]{2,1,0:T(8,128)(2,1)S(1)} %get-tuple-element.8.far_ref, bf16[256,1024]{1,0:T(8,128)(2,1)S(1)} %get-tuple-element.9.near_mats_ref, bf16[256,5120]{1,0:T(8,128)(2,1)S(1)} %get-tuple-element.10.pick_ref), custom_call_target="tpu_custom_call" | custom-call | flops 1400000000 | bytes 6000000 | tf_op jit(solution)/shard_map/field/pallas_call | solution.py:166
  35.6 18.0 %all_to_all.11 = bf16[128,4,128]{2,1,0:T(4,128)(2,1)S(1)} all-to-all(bf16[128,4,128]{2,1,0:T(4,128)(2,1)S(1)} %bitcast.13), channel_id=1, replica_groups={{72,73,74,75,76,77,78,79,64,65,66,67,68,69,70,71,88,89,90,91,92,93,94,9..., dimensions={0} | all-to-all | bytes 262144 | tf_op jit(solution)/shard_map/all_to_all | solution.py:21
  53.6 0.7 %whole.1 = bf16[2,8,2,8,2,128]{5,4,3,2,1,0:T(2,128)(2,1)} custom-call(bf16[8,2,8,2,2,128]{5,4,3,2,1,0:T(2,128)(2,1)S(1)} %bitcast.10), custom_call_target="tpu_custom_call" | custom-call | tf_op jit(solution)/shard_map/whole/pallas_call | solution.py:187
Async XLA Ops:
  0.0 0.9 %copy-start = (bf16[2,256,128]{2,1,0:T(8,128)(2,1)S(1)}, bf16[2,256,128]{2,1,0:T(8,128)(2,1)}, u32[]{:S(2)}) copy-start(bf16[2,256,128]{2,1,0:T(8,128)(2,1)} %param.5) | copy-start | bytes 393220
  26.8 7.2 %collective-permute-start = (bf16[128,4,128]{2,1,0:T(4,128)(2,1)S(1)}, bf16[128,4,128]{2,1,0:T(4,128)(2,1)S(1)}, u32[]{:S(2)}, u32[]{:S(2)}) collective-permute-start(bf16[128,4,128]{2,1,0:T(4,128)(2,1)S(1)} %all_to_all.10._), channel_id=1, source_target_pairs={{0,128},{128,256},{256,384},{1,129},{129,257},{257,385},{2,130},{1... | collective-permute-start | bytes 393224 | tf_op jit(solution)/shard_map/ppermute | solution.py:145
  29.9 0.7 %copy-start.1 = (s32[256,12]{0,1:T(8,128)S(1)}, s32[256,12]{0,1:T(8,128)}, u32[]{:S(2)}) copy-start(s32[256,12]{0,1:T(8,128)} %param.6) | copy-start | bytes 36868
  30.6 0.7 %copy-start.2 = (f32[12,2,128]{2,1,0:T(2,128)S(1)}, f32[12,2,128]{2,1,0:T(2,128)}, u32[]{:S(2)}) copy-start(f32[12,2,128]{2,1,0:T(2,128)} %trans_ref.1) | copy-start | bytes 36868
  31.3 0.7 %copy-start.3 = (s32[256,8]{0,1:T(8,128)S(1)}, s32[256,8]{0,1:T(8,128)}, u32[]{:S(2)}) copy-start(s32[256,8]{0,1:T(8,128)} %param.7) | copy-start | bytes 24580
  32.0 0.7 %copy-start.4 = (f32[8,128]{1,0:T(8,128)S(1)}, f32[8,128]{1,0:T(8,128)}, u32[]{:S(2)}) copy-start(f32[8,128]{1,0:T(8,128)} %slot_ref.1) | copy-start | bytes 12292

commit v2 on v1

v2 whole, which is shorter than its diff:
```python
import functools

import jax
import jax.numpy as jnp
from jax import lax
from jax.experimental import pallas as pl
from jax.experimental.pallas import tpu as pltpu
from jax.sharding import PartitionSpec as P

VMEM = pl.BlockSpec(memory_space=pltpu.VMEM)
HBM = pl.BlockSpec(memory_space=pltpu.HBM)
Z, Y, CORES = 8, 8, 2
BATCH = Y // 2 * CORES


def in_hbm(array):
    return pltpu.with_memory_space_constraint(array, pltpu.HBM)


def ranks():
    return [((z + Z // 2) % Z * Y + (y + Y // 2) % Y) * CORES + c for z in range(Z) for y in range(Y) for c in range(CORES)]


def exchange(chunks):
    return lax.all_to_all(chunks, "space", split_axis=0, concat_axis=0, axis_index_groups=[ranks()], tiled=True)


def turned(box, z_half, y_half):
    half = Z // 2
    own = (box, pl.ds(z_half * half, half), y_half)
    there = (pl.ds((1 - z_half) * half, half), 1 - y_half, slice(None), box)
    return own, there


def parts_kernel(signal_ref, parts_ref, sems):
    copies = []
    for n in range(signal_ref.shape[0] * 4):
        own, there = turned(n // 4, n // 2 % 2, n % 2)
        copies.append(pltpu.make_async_copy(signal_ref.at[own], parts_ref.at[there], sems.at[n]))
    for copy in copies:
        copy.start()
    for copy in copies:
        copy.wait()


def whole_kernel(parts_ref, field_ref, sems):
    copies = []
    for n in range(field_ref.shape[0] * 4):
        own, there = turned(n // 4, n // 2 % 2, n % 2)
        copies.append(pltpu.make_async_copy(parts_ref.at[there], field_ref.at[own], sems.at[n]))
    for copy in copies:
        copy.start()
    for copy in copies:
        copy.wait()


def circulant_halves(lags):
    width = lags.shape[-1]
    lags = lags.astype(jnp.bfloat16).astype(jnp.float32)
    turned = pltpu.roll(jnp.broadcast_to(lags, (width, width)), 0, 1, stride=1, stride_axis=0)
    s = lax.broadcasted_iota(jnp.int32, (width, width), 0)
    t = lax.broadcasted_iota(jnp.int32, (width, width), 1)
    before = jnp.where(t < s, turned, 0.0).astype(jnp.bfloat16)
    within = jnp.where(t >= s, turned, 0.0).astype(jnp.bfloat16)
    return before, within


def rows_of_rays(block_ref, wide, rows):
    rays, boxes, _ = rows.shape
    wide[...] = block_ref[...].astype(jnp.float32)
    for r in range(rays):
        rows[r] = wide[pl.ds(r, boxes, stride=rays), :].astype(jnp.bfloat16)


def mix(rows, far_ref, slot_ref, mixed):
    rays, boxes, width = rows.shape
    offsets, slots = far_ref.shape[2] // width, slot_ref.shape[1] // width
    for r in range(rays):
        own = rows[r]
        lanes = slice(r * width, (r + 1) * width)
        for k in range(0, offsets + slots, 2):
            if k < offsets:
                mats = far_ref[r, :, k * width : (k + 2) * width]
            else:
                mats = slot_ref[:, (k - offsets) * width : (k - offsets + 2) * width]
            two = jnp.dot(own, mats, preferred_element_type=jnp.float32).astype(jnp.bfloat16)
            mixed[k * boxes : (k + 1) * boxes, lanes] = two[:, :width]
            mixed[(k + 1) * boxes : (k + 2) * boxes, lanes] = two[:, width:]


def pick(pick_ref, mixed, cut):
    far = jnp.dot(pick_ref[:, :cut], mixed[:cut, :], preferred_element_type=jnp.float32)
    near = jnp.dot(pick_ref[:, cut:], mixed[cut:, :], preferred_element_type=jnp.float32)
    return far, near


def current_kernel(
    source_hbm, near_hbm, trans_hbm, slot_hbm, cur_ref, far_before, slot_before, pick_ref, sums_ref,
    source_ref, near_ref, trans_ref, slot_ref, sems, far_within, slot_within, wide, rows, mixed,
):
    given, held = (source_hbm, near_hbm, trans_hbm, slot_hbm), (source_ref, near_ref, trans_ref, slot_ref)
    copies = [pltpu.make_async_copy(ref, here, sems.at[n]) for n, (ref, here) in enumerate(zip(given, held))]
    for copy in copies:
        copy.start()
    rows_of_rays(cur_ref, wide, rows)
    for copy in copies:
        copy.wait()
    offsets, rays, width = trans_ref.shape
    slots = slot_ref.shape[0]
    boxes = source_ref.shape[1]
    for k in range(offsets):
        for r in range(rays):
            before, within = circulant_halves(trans_ref[k, r : r + 1, :])
            far_before[r, :, k * width : (k + 1) * width] = before
            far_within[r, :, k * width : (k + 1) * width] = within
    for j in range(slots):
        before, within = circulant_halves(slot_ref[j : j + 1, :])
        slot_before[:, j * width : (j + 1) * width] = before
        slot_within[:, j * width : (j + 1) * width] = within
    per_dev = boxes // (Z * Y * CORES)
    y_turn, z_turn = BATCH * per_dev, boxes // 2
    lane = lax.broadcasted_iota(jnp.int32, (boxes, boxes), 1) ^ (y_turn | z_turn)

    def by_rank(columns):
        runs = [(p ^ (y_turn | z_turn)) for p in range(0, boxes, y_turn)]
        return jnp.concatenate([columns[p : p + y_turn] for p in runs], axis=0)

    source = by_rank(jnp.transpose(source_ref[...]))
    near = by_rank(jnp.transpose(near_ref[...]))
    for k in range(offsets + slots):
        column = source[:, k : k + 1] if k < offsets else near[:, k - offsets : k - offsets + 1]
        hit = jnp.where(column == lane, 1.0, 0.0)
        pick_ref[:, k * boxes : (k + 1) * boxes] = hit.astype(jnp.bfloat16)
    mix(rows, far_within, slot_within, mixed)
    sums_ref[0], sums_ref[1] = pick(pick_ref, mixed, offsets * boxes)


def earlier_kernel(prev_ref, far_before, slot_before, pick_ref, sums_ref, out_ref, wide, rows, mixed):
    rays, width, far_cols = far_before.shape
    boxes = pick_ref.shape[0]
    rows_of_rays(prev_ref, wide, rows)
    mix(rows, far_before, slot_before, mixed)
    far, near = pick(pick_ref, mixed, far_cols // width * boxes)
    far = (sums_ref[0] + far).astype(jnp.bfloat16).astype(jnp.float32)
    near = (sums_ref[1] + near).astype(jnp.bfloat16).astype(jnp.float32)
    both = far + near
    for r in range(rays):
        wide[pl.ds(r, boxes, stride=rays), :] = both[:, r * width : (r + 1) * width]
    out_ref[...] = wide[...].astype(jnp.bfloat16)


def body(signal, source_boxes, near_boxes, trans_kernel, near_kernel):
    box_dev, all_rays, width = signal.shape
    devs = lax.axis_size("space")
    rays = all_rays // devs
    boxes = box_dev * devs
    offsets, slots = trans_kernel.shape[0], near_kernel.shape[0]
    mid = box_dev * rays

    split = (box_dev, Z, 2, BATCH, rays, width)
    parted = pl.pallas_call(
        parts_kernel,
        out_shape=jax.ShapeDtypeStruct((Z, 2, BATCH, box_dev, rays, width), signal.dtype),
        in_specs=[HBM],
        out_specs=VMEM,
        scratch_shapes=[pltpu.SemaphoreType.DMA((4 * box_dev,))],
        compiler_params=pltpu.CompilerParams(vmem_limit_bytes=4 << 20),
        name="parts",
    )(in_hbm(signal.reshape(split)))
    current = exchange(parted.reshape(devs, mid, width))
    size = lax.axis_size("tm")
    earlier = lax.ppermute(current, "tm", [(i, i + 1) for i in range(size - 1)])

    far_before = jax.ShapeDtypeStruct((rays, width, offsets * width), jnp.bfloat16)
    slot_before = jax.ShapeDtypeStruct((width, slots * width), jnp.bfloat16)
    work = [
        pltpu.VMEM((devs * mid, width), jnp.float32),
        pltpu.VMEM((rays, boxes, width), jnp.bfloat16),
        pltpu.VMEM(((offsets + slots) * boxes, rays * width), jnp.bfloat16),
    ]
    begun = pl.pallas_call(
        current_kernel,
        out_shape=(
            far_before,
            slot_before,
            jax.ShapeDtypeStruct((boxes, (offsets + slots) * boxes), jnp.bfloat16),
            jax.ShapeDtypeStruct((2, boxes, rays * width), jnp.float32),
        ),
        in_specs=[HBM] * 4 + [VMEM],
        out_specs=(VMEM,) * 4,
        scratch_shapes=[
            pltpu.VMEM((offsets, boxes), jnp.int32),
            pltpu.VMEM((slots, boxes), jnp.int32),
            pltpu.VMEM(trans_kernel.shape, jnp.float32),
            pltpu.VMEM(near_kernel.shape, jnp.float32),
            pltpu.SemaphoreType.DMA((4,)),
            pltpu.VMEM(far_before.shape, jnp.bfloat16),
            pltpu.VMEM(slot_before.shape, jnp.bfloat16),
            *work,
        ],
        compiler_params=pltpu.CompilerParams(vmem_limit_bytes=24 << 20),
        cost_estimate=pl.CostEstimate(flops=1_000_000_000, bytes_accessed=6_000_000, transcendentals=0),
        name="current",
    )(
        in_hbm(source_boxes.T),
        in_hbm(near_boxes.T),
        in_hbm(trans_kernel),
        in_hbm(near_kernel),
        current.reshape(devs * mid, width),
    )
    field = pl.pallas_call(
        earlier_kernel,
        out_shape=jax.ShapeDtypeStruct((devs * mid, width), jnp.bfloat16),
        in_specs=[VMEM] * 5,
        out_specs=VMEM,
        scratch_shapes=work,
        compiler_params=pltpu.CompilerParams(vmem_limit_bytes=24 << 20),
        cost_estimate=pl.CostEstimate(flops=1_000_000_000, bytes_accessed=6_000_000, transcendentals=0),
        name="earlier",
    )(earlier.reshape(devs * mid, width), *begun)
    back = exchange(field.reshape(devs, mid, width))
    whole = pl.pallas_call(
        whole_kernel,
        out_shape=jax.ShapeDtypeStruct(split, signal.dtype),
        in_specs=[VMEM],
        out_specs=pl.BlockSpec(memory_space=pl.ANY),
        scratch_shapes=[pltpu.SemaphoreType.DMA((4 * box_dev,))],
        compiler_params=pltpu.CompilerParams(vmem_limit_bytes=4 << 20),
        name="whole",
    )(back.reshape(Z, 2, BATCH, box_dev, rays, width))
    return whole.reshape(signal.shape)


def solution(mesh):
    in_specs = (P("space", None, "tm"), P(), P(), P(None, "space", None), P())
    out_specs = P("space", None, "tm")
    return jax.shard_map(body, mesh=mesh, in_specs=in_specs, out_specs=out_specs, check_vma=False)
```

time: 54.8 us -> 53.5 us (0.976)
  local copies, waits for them, and re-layouts: 3.71 us -> 0 us
  Pallas kernels: 3.74 us -> 5.95 us
    unnamed x10 -> x0, local copies, waits for them, and re-layouts: 3.71 us -> none
    pallas_call x2, Pallas kernels: 2.85 us -> 4.34 us  [the longest x1 2.77 us: body(): pl.pallas_call(current_kernel, out_shape=(far_before, slot_before, jax.Sh...]
    pallas_call x1, Pallas kernels: 0.18 us -> 0.9 us  [body(): pl.pallas_call(parts_kernel, out_shape=jax.ShapeDtypeStruct((Z, 2, BATCH,...]
  transfers between devices with their start and end apart: 1 -> 1, of which waited for: 0 -> 0; matrix products, arithmetic and copies ran while one was open for 0% -> 0% of each run, Pallas kernels for 2% -> 5%
where the time goes in v2:
time: 53.5 us; the launch traced here: 53 us
  blocking collectives  43.9 us (82%)
  Pallas kernels  5.95 us (11%)
  starting transfers between devices  3.11 us (6%)
    all_to_all x2, blocking collectives, exchange(): lax.all_to_all(chunks, 'space', split_axis=0, concat_axis=0, axis_index_g...  43.9 us
    ppermute x1, starting transfers between devices, body(): earlier = lax.ppermute(current, 'tm', [(i, i + 1) for i in range(size - 1)])  3.11 us
    pallas_call x1, Pallas kernels, body(): pl.pallas_call(current_kernel, out_shape=(far_before, slot_before, jax.Sh...  2.77 us
    pallas_call x1, Pallas kernels, body(): pl.pallas_call(earlier_kernel, out_shape=jax.ShapeDtypeStruct((devs * mid...  1.56 us
  transfers between devices with their start and end apart: 1, of which 0 were waited for; matrix products, arithmetic and copies ran while one was open for 0% of the time, Pallas kernels for 5%

profile of v2, /device:TPU:1, one launch (start us, length us, event | category | flops | bytes accessed | tf_op | source)
XLA Modules:
  0.0 53.0 jit_solution(16477169318851211873)
XLA Ops:
  0.0 0.9 %parts.1 = bf16[8,2,8,2,2,128]{5,4,3,2,1,0:T(2,128)(2,1)S(1)} custom-call(bf16[2,8,2,8,2,128]{5,4,3,2,1,0:T(2,128)(2,1)} %bitcast.14), custom_call_target="tpu_custom_call" | custom-call | tf_op jit(solution)/shard_map/parts/pallas_call | solution.py:161
  0.9 25.7 %all_to_all.10 = bf16[128,4,128]{2,1,0:T(4,128)(2,1)S(1)} all-to-all(bf16[128,4,128]{2,1,0:T(4,128)(2,1)S(1)} %bitcast.11), channel_id=1, replica_groups={{72,73,74,75,76,77,78,79,64,65,66,67,68,69,70,71,88,89,90,91,92,93,94,9..., dimensions={0} | all-to-all | bytes 262144 | tf_op jit(solution)/shard_map/all_to_all | solution.py:25
  26.6 3.1 %collective-permute-start = (bf16[128,4,128]{2,1,0:T(4,128)(2,1)S(1)}, bf16[128,4,128]{2,1,0:T(4,128)(2,1)S(1)}, u32[]{:S(2)}, u32[]{:S(2)}) collective-permute-start(bf16[128,4,128]{2,1,0:T(4,128)(2,1)S(1)} %all_to_all.10), channel_id=1, source_target_pairs={{0,128},{128,256},{256,384},{1,129},{129,257},{257,385},{2,130},{1... | collective-permute-start | bytes 393224 | tf_op jit(solution)/shard_map/ppermute | solution.py:172
  29.7 2.8 %current.1 = (bf16[2,128,1536]{2,1,0:T(8,128)(2,1)S(1)}, bf16[128,1024]{1,0:T(8,128)(2,1)S(1)}, bf16[256,5120]{1,0:T(8,128)(2,1)S(1)}, f32[2,256,256]{2,1,0:T(8,128)S(1)}) custom-call(s32[12,256]{1,0:T(8,128)} %bitcast.15, s32[8,256]{1,0:T(8,128)} %bitcast.16, f32[12,2,128]{2,1,0:T(2,128)} %trans_hbm.1, f32[8,128]{1,0:T(8,128)} %slot_hbm.1, ...), custom_call_target="tpu_custom_call" | custom-call | flops 1000000000 | bytes 6000000 | tf_op jit(solution)/shard_map/current/pallas_call | solution.py:181
  32.5 0.0 collective-permute-done
  32.5 1.6 %earlier.1 = bf16[512,128]{1,0:T(8,128)(2,1)S(1)} custom-call(bf16[512,128]{1,0:T(8,128)(2,1)S(1)} %bitcast.12, bf16[2,128,1536]{2,1,0:T(8,128)(2,1)S(1)} %get-tuple-element.9.far_before, bf16[128,1024]{1,0:T(8,128)(2,1)S(1)} %get-tuple-element.10.slot_before, bf16[256,5120]{1,0:T(8,128)(2,1)S(1)} %get-tuple-element.11.pick_ref, ...), custom_call_target="tpu_custom_call" | custom-call | flops 1000000000 | bytes 6000000 | tf_op jit(solution)/shard_map/earlier/pallas_call | solution.py:211
  34.1 18.2 %all_to_all.11 = bf16[128,4,128]{2,1,0:T(4,128)(2,1)S(1)} all-to-all(bf16[128,4,128]{2,1,0:T(4,128)(2,1)S(1)} %bitcast.9), channel_id=1, replica_groups={{72,73,74,75,76,77,78,79,64,65,66,67,68,69,70,71,88,89,90,91,92,93,94,9..., dimensions={0} | all-to-all | bytes 262144 | tf_op jit(solution)/shard_map/all_to_all | solution.py:25
  52.3 0.7 %whole.1 = bf16[2,8,2,8,2,128]{5,4,3,2,1,0:T(2,128)(2,1)} custom-call(bf16[8,2,8,2,2,128]{5,4,3,2,1,0:T(2,128)(2,1)S(1)} %bitcast.10), custom_call_target="tpu_custom_call" | custom-call | tf_op jit(solution)/shard_map/whole/pallas_call | solution.py:222
Async XLA Ops:
  26.6 5.9 %collective-permute-start = (bf16[128,4,128]{2,1,0:T(4,128)(2,1)S(1)}, bf16[128,4,128]{2,1,0:T(4,128)(2,1)S(1)}, u32[]{:S(2)}, u32[]{:S(2)}) collective-permute-start(bf16[128,4,128]{2,1,0:T(4,128)(2,1)S(1)} %all_to_all.10), channel_id=1, source_target_pairs={{0,128},{128,256},{256,384},{1,129},{129,257},{257,385},{2,130},{1... | collective-permute-start | bytes 393224 | tf_op jit(solution)/shard_map/ppermute | solution.py:172

commit v3 on v2

--- a/solution.py
+++ b/solution.py
@@ -10,48 +10,35 @@
 VMEM = pl.BlockSpec(memory_space=pltpu.VMEM)
 HBM = pl.BlockSpec(memory_space=pltpu.HBM)
 Z, Y, CORES = 8, 8, 2
-BATCH = Y // 2 * CORES
+TURNS = (4, 0, 6, 2, 5, 1, 7, 3)
+CHIPS = [z * Y + y for y in TURNS for z in TURNS]
+RANKS = [chip * CORES + c for chip in CHIPS for c in range(CORES)]
 
 
 def in_hbm(array):
     return pltpu.with_memory_space_constraint(array, pltpu.HBM)
 
 
-def ranks():
-    return [((z + Z // 2) % Z * Y + (y + Y // 2) % Y) * CORES + c for z in range(Z) for y in range(Y) for c in range(CORES)]
-
-
 def exchange(chunks):
-    return lax.all_to_all(chunks, "space", split_axis=0, concat_axis=0, axis_index_groups=[ranks()], tiled=True)
-
-
-def turned(box, z_half, y_half):
-    half = Z // 2
-    own = (box, pl.ds(z_half * half, half), y_half)
-    there = (pl.ds((1 - z_half) * half, half), 1 - y_half, slice(None), box)
-    return own, there
-
-
-def parts_kernel(signal_ref, parts_ref, sems):
-    copies = []
-    for n in range(signal_ref.shape[0] * 4):
-        own, there = turned(n // 4, n // 2 % 2, n % 2)
-        copies.append(pltpu.make_async_copy(signal_ref.at[own], parts_ref.at[there], sems.at[n]))
-    for copy in copies:
-        copy.start()
-    for copy in copies:
-        copy.wait()
-
-
-def whole_kernel(parts_ref, field_ref, sems):
-    copies = []
-    for n in range(field_ref.shape[0] * 4):
-        own, there = turned(n // 4, n // 2 % 2, n % 2)
-        copies.append(pltpu.make_async_copy(parts_ref.at[there], field_ref.at[own], sems.at[n]))
-    for copy in copies:
-        copy.start()
-    for copy in copies:
-        copy.wait()
+    return lax.all_to_all(chunks, "space", split_axis=0, concat_axis=0, axis_index_groups=[RANKS], tiled=True)
+
+
+def parts_kernel(signal_hbm, parts_ref, signal_ref, sem):
+    copy = pltpu.make_async_copy(signal_hbm, signal_ref, sem)
+    copy.start()
+    copy.wait()
+    for rank, dev in enumerate(RANKS):
+        for box in range(signal_ref.shape[0]):
+            parts_ref[rank, box] = signal_ref[box, dev]
+
+
+def whole_kernel(parts_ref, field_hbm, field_ref, sem):
+    for rank, dev in enumerate(RANKS):
+        for box in range(field_ref.shape[0]):
+            field_ref[box, dev] = parts_ref[rank, box]
+    copy = pltpu.make_async_copy(field_ref, field_hbm, sem)
+    copy.start()
+    copy.wait()
 
 
 def circulant_halves(lags):
@@ -67,7 +54,11 @@
 
 def rows_of_rays(block_ref, wide, rows):
     rays, boxes, _ = rows.shape
-    wide[...] = block_ref[...].astype(jnp.float32)
+    run = wide.shape[0] // len(CHIPS)
+    for n in range(0, len(CHIPS), 2):
+        two = block_ref[n * run : (n + 2) * run, :].astype(jnp.float32)
+        for chip, one in ((CHIPS[n], two[:run]), (CHIPS[n + 1], two[run:])):
+            wide[chip * run : (chip + 1) * run, :] = one
     for r in range(rays):
         rows[r] = wide[pl.ds(r, boxes, stride=rays), :].astype(jnp.bfloat16)
 
@@ -117,16 +108,9 @@
         before, within = circulant_halves(slot_ref[j : j + 1, :])
         slot_before[:, j * width : (j + 1) * width] = before
         slot_within[:, j * width : (j + 1) * width] = within
-    per_dev = boxes // (Z * Y * CORES)
-    y_turn, z_turn = BATCH * per_dev, boxes // 2
-    lane = lax.broadcasted_iota(jnp.int32, (boxes, boxes), 1) ^ (y_turn | z_turn)
-
-    def by_rank(columns):
-        runs = [(p ^ (y_turn | z_turn)) for p in range(0, boxes, y_turn)]
-        return jnp.concatenate([columns[p : p + y_turn] for p in runs], axis=0)
-
-    source = by_rank(jnp.transpose(source_ref[...]))
-    near = by_rank(jnp.transpose(near_ref[...]))
+    lane = lax.broadcasted_iota(jnp.int32, (boxes, boxes), 1)
+    source = jnp.transpose(source_ref[...])
+    near = jnp.transpose(near_ref[...])
     for k in range(offsets + slots):
         column = source[:, k : k + 1] if k < offsets else near[:, k - offsets : k - offsets + 1]
         hit = jnp.where(column == lane, 1.0, 0.0)
@@ -146,7 +130,10 @@
     both = far + near
     for r in range(rays):
         wide[pl.ds(r, boxes, stride=rays), :] = both[:, r * width : (r + 1) * width]
-    out_ref[...] = wide[...].astype(jnp.bfloat16)
+    run = wide.shape[0] // len(CHIPS)
+    for n in range(0, len(CHIPS), 2):
+        two = [wide[chip * run : (chip + 1) * run, :] for chip in CHIPS[n : n + 2]]
+        out_ref[n * run : (n + 2) * run, :] = jnp.concatenate(two, axis=0).astype(jnp.bfloat16)
 
 
 def body(signal, source_boxes, near_boxes, trans_kernel, near_kernel):
@@ -157,13 +144,13 @@
     offsets, slots = trans_kernel.shape[0], near_kernel.shape[0]
     mid = box_dev * rays
 
-    split = (box_dev, Z, 2, BATCH, rays, width)
+    split = (box_dev, devs, rays, width)
     parted = pl.pallas_call(
         parts_kernel,
-        out_shape=jax.ShapeDtypeStruct((Z, 2, BATCH, box_dev, rays, width), signal.dtype),
+        out_shape=jax.ShapeDtypeStruct((devs, box_dev, rays, width), signal.dtype),
         in_specs=[HBM],
         out_specs=VMEM,
-        scratch_shapes=[pltpu.SemaphoreType.DMA((4 * box_dev,))],
+        scratch_shapes=[pltpu.VMEM(split, signal.dtype), pltpu.SemaphoreType.DMA],
         compiler_params=pltpu.CompilerParams(vmem_limit_bytes=4 << 20),
         name="parts",
     )(in_hbm(signal.reshape(split)))
@@ -224,10 +211,10 @@
         out_shape=jax.ShapeDtypeStruct(split, signal.dtype),
         in_specs=[VMEM],
         out_specs=pl.BlockSpec(memory_space=pl.ANY),
-        scratch_shapes=[pltpu.SemaphoreType.DMA((4 * box_dev,))],
+        scratch_shapes=[pltpu.VMEM(split, signal.dtype), pltpu.SemaphoreType.DMA],
         compiler_params=pltpu.CompilerParams(vmem_limit_bytes=4 << 20),
         name="whole",
-    )(back.reshape(Z, 2, BATCH, box_dev, rays, width))
+    )(back.reshape(devs, box_dev, rays, width))
     return whole.reshape(signal.shape)
 
 

time: 53.5 us -> 52.8 us (0.987)
  blocking collectives: 43.9 us -> 43.1 us
    all_to_all x2, blocking collectives: 43.9 us -> 43.1 us  [exchange(): lax.all_to_all(chunks, 'space', split_axis=0, concat_axis=0, axis_index_g...]
where the time goes in v3:
time: 52.8 us; the launch traced here: 52.4 us
  blocking collectives  43.1 us (82%)
  Pallas kernels  6.1 us (12%)
  starting transfers between devices  3.11 us (6%)
    all_to_all x2, blocking collectives, exchange(): lax.all_to_all(chunks, 'space', split_axis=0, concat_axis=0, axis_index_g...  43.1 us
    ppermute x1, starting transfers between devices, body(): earlier = lax.ppermute(current, 'tm', [(i, i + 1) for i in range(size - 1)])  3.11 us
    pallas_call x1, Pallas kernels, body(): pl.pallas_call(current_kernel, out_shape=(far_before, slot_before, jax.Sh...  2.79 us
    pallas_call x1, Pallas kernels, body(): pl.pallas_call(earlier_kernel, out_shape=jax.ShapeDtypeStruct((devs * mid...  1.56 us
  transfers between devices with their start and end apart: 1, of which 0 were waited for; matrix products, arithmetic and copies ran while one was open for 0% of the time, Pallas kernels for 5%

profile of v3, /device:TPU:1, one launch (start us, length us, event | category | flops | bytes accessed | tf_op | source)
XLA Modules:
  0.0 52.4 jit_solution(4501493743957182696)
XLA Ops:
  0.0 1.0 %parts.1 = bf16[128,2,2,128]{3,2,1,0:T(2,128)(2,1)S(1)} custom-call(bf16[2,128,2,128]{3,2,1,0:T(2,128)(2,1)} %bitcast.14), custom_call_target="tpu_custom_call" | custom-call | tf_op jit(solution)/shard_map/parts/pallas_call | solution.py:148
  1.0 25.4 %all_to_all.10 = bf16[128,4,128]{2,1,0:T(4,128)(2,1)S(1)} all-to-all(bf16[128,4,128]{2,1,0:T(4,128)(2,1)S(1)} %bitcast.11), channel_id=1, replica_groups={{72,73,8,9,104,105,40,41,88,89,24,25,120,121,56,57,64,65,0,1,96,97,32,3..., dimensions={0} | all-to-all | bytes 262144 | tf_op jit(solution)/shard_map/all_to_all | solution.py:23
  26.4 3.1 %collective-permute-start = (bf16[128,4,128]{2,1,0:T(4,128)(2,1)S(1)}, bf16[128,4,128]{2,1,0:T(4,128)(2,1)S(1)}, u32[]{:S(2)}, u32[]{:S(2)}) collective-permute-start(bf16[128,4,128]{2,1,0:T(4,128)(2,1)S(1)} %all_to_all.10), channel_id=1, source_target_pairs={{0,128},{128,256},{256,384},{1,129},{129,257},{257,385},{2,130},{1... | collective-permute-start | bytes 393224 | tf_op jit(solution)/shard_map/ppermute | solution.py:159
  29.6 2.8 %current.1 = (bf16[2,128,1536]{2,1,0:T(8,128)(2,1)S(1)}, bf16[128,1024]{1,0:T(8,128)(2,1)S(1)}, bf16[256,5120]{1,0:T(8,128)(2,1)S(1)}, f32[2,256,256]{2,1,0:T(8,128)S(1)}) custom-call(s32[12,256]{1,0:T(8,128)} %bitcast.15, s32[8,256]{1,0:T(8,128)} %bitcast.16, f32[12,2,128]{2,1,0:T(2,128)} %trans_hbm.1, f32[8,128]{1,0:T(8,128)} %slot_hbm.1, ...), custom_call_target="tpu_custom_call" | custom-call | flops 1000000000 | bytes 6000000 | tf_op jit(solution)/shard_map/current/pallas_call | solution.py:168
  32.3 0.0 collective-permute-done
  32.4 1.6 %earlier.1 = bf16[512,128]{1,0:T(8,128)(2,1)S(1)} custom-call(bf16[512,128]{1,0:T(8,128)(2,1)S(1)} %bitcast.12, bf16[2,128,1536]{2,1,0:T(8,128)(2,1)S(1)} %get-tuple-element.9.far_before, bf16[128,1024]{1,0:T(8,128)(2,1)S(1)} %get-tuple-element.10.slot_before, bf16[256,5120]{1,0:T(8,128)(2,1)S(1)} %get-tuple-element.11.pick_ref, ...), custom_call_target="tpu_custom_call" | custom-call | flops 1000000000 | bytes 6000000 | tf_op jit(solution)/shard_map/earlier/pallas_call | solution.py:198
  33.9 17.7 %all_to_all.11 = bf16[128,4,128]{2,1,0:T(4,128)(2,1)S(1)} all-to-all(bf16[128,4,128]{2,1,0:T(4,128)(2,1)S(1)} %bitcast.9), channel_id=1, replica_groups={{72,73,8,9,104,105,40,41,88,89,24,25,120,121,56,57,64,65,0,1,96,97,32,3..., dimensions={0} | all-to-all | bytes 262144 | tf_op jit(solution)/shard_map/all_to_all | solution.py:23
  51.6 0.8 %whole.1 = bf16[2,128,2,128]{3,2,1,0:T(2,128)(2,1)} custom-call(bf16[128,2,2,128]{3,2,1,0:T(2,128)(2,1)S(1)} %bitcast.10), custom_call_target="tpu_custom_call" | custom-call | tf_op jit(solution)/shard_map/whole/pallas_call | solution.py:209
Async XLA Ops:
  26.4 5.9 %collective-permute-start = (bf16[128,4,128]{2,1,0:T(4,128)(2,1)S(1)}, bf16[128,4,128]{2,1,0:T(4,128)(2,1)S(1)}, u32[]{:S(2)}, u32[]{:S(2)}) collective-permute-start(bf16[128,4,128]{2,1,0:T(4,128)(2,1)S(1)} %all_to_all.10), channel_id=1, source_target_pairs={{0,128},{128,256},{256,384},{1,129},{129,257},{257,385},{2,130},{1... | collective-permute-start | bytes 393224 | tf_op jit(solution)/shard_map/ppermute | solution.py:159

commit v4 on v3

--- a/solution.py
+++ b/solution.py
@@ -63,31 +63,28 @@
         rows[r] = wide[pl.ds(r, boxes, stride=rays), :].astype(jnp.bfloat16)
 
 
-def mix(rows, far_ref, slot_ref, mixed):
+def sums_of(rows, far_ref, slot_ref, pick_ref, taken):
     rays, boxes, width = rows.shape
-    offsets, slots = far_ref.shape[2] // width, slot_ref.shape[1] // width
-    for r in range(rays):
-        own = rows[r]
-        lanes = slice(r * width, (r + 1) * width)
-        for k in range(0, offsets + slots, 2):
-            if k < offsets:
-                mats = far_ref[r, :, k * width : (k + 2) * width]
-            else:
-                mats = slot_ref[:, (k - offsets) * width : (k - offsets + 2) * width]
-            two = jnp.dot(own, mats, preferred_element_type=jnp.float32).astype(jnp.bfloat16)
-            mixed[k * boxes : (k + 1) * boxes, lanes] = two[:, :width]
-            mixed[(k + 1) * boxes : (k + 2) * boxes, lanes] = two[:, width:]
-
-
-def pick(pick_ref, mixed, cut):
-    far = jnp.dot(pick_ref[:, :cut], mixed[:cut, :], preferred_element_type=jnp.float32)
-    near = jnp.dot(pick_ref[:, cut:], mixed[cut:, :], preferred_element_type=jnp.float32)
-    return far, near
+    offsets, slots = far_ref.shape[1] // width, slot_ref.shape[0] // width
+    beside = jnp.concatenate([rows[r] for r in range(rays)], axis=1)
+    for k in range(offsets + slots):
+        got = jnp.dot(pick_ref[k * boxes : (k + 1) * boxes, :], beside, preferred_element_type=jnp.float32)
+        got = got.astype(jnp.bfloat16)
+        for r in range(rays):
+            taken[r, :, k * width : (k + 1) * width] = got[:, r * width : (r + 1) * width]
+    cut = offsets * width
+    return [
+        (
+            jnp.dot(taken[r, :, :cut], far_ref[r], preferred_element_type=jnp.float32),
+            jnp.dot(taken[r, :, cut:], slot_ref[...], preferred_element_type=jnp.float32),
+        )
+        for r in range(rays)
+    ]
 
 
 def current_kernel(
     source_hbm, near_hbm, trans_hbm, slot_hbm, cur_ref, far_before, slot_before, pick_ref, sums_ref,
-    source_ref, near_ref, trans_ref, slot_ref, sems, far_within, slot_within, wide, rows, mixed,
+    source_ref, near_ref, trans_ref, slot_ref, sems, far_within, slot_within, wide, rows, taken,
 ):
     given, held = (source_hbm, near_hbm, trans_hbm, slot_hbm), (source_ref, near_ref, trans_ref, slot_ref)
     copies = [pltpu.make_async_copy(ref, here, sems.at[n]) for n, (ref, here) in enumerate(zip(given, held))]
@@ -102,34 +99,30 @@
     for k in range(offsets):
         for r in range(rays):
             before, within = circulant_halves(trans_ref[k, r : r + 1, :])
-            far_before[r, :, k * width : (k + 1) * width] = before
-            far_within[r, :, k * width : (k + 1) * width] = within
+            far_before[r, k * width : (k + 1) * width, :] = before
+            far_within[r, k * width : (k + 1) * width, :] = within
     for j in range(slots):
         before, within = circulant_halves(slot_ref[j : j + 1, :])
-        slot_before[:, j * width : (j + 1) * width] = before
-        slot_within[:, j * width : (j + 1) * width] = within
+        slot_before[j * width : (j + 1) * width, :] = before
+        slot_within[j * width : (j + 1) * width, :] = within
     lane = lax.broadcasted_iota(jnp.int32, (boxes, boxes), 1)
     source = jnp.transpose(source_ref[...])
     near = jnp.transpose(near_ref[...])
     for k in range(offsets + slots):
         column = source[:, k : k + 1] if k < offsets else near[:, k - offsets : k - offsets + 1]
         hit = jnp.where(column == lane, 1.0, 0.0)
-        pick_ref[:, k * boxes : (k + 1) * boxes] = hit.astype(jnp.bfloat16)
-    mix(rows, far_within, slot_within, mixed)
-    sums_ref[0], sums_ref[1] = pick(pick_ref, mixed, offsets * boxes)
-
-
-def earlier_kernel(prev_ref, far_before, slot_before, pick_ref, sums_ref, out_ref, wide, rows, mixed):
-    rays, width, far_cols = far_before.shape
-    boxes = pick_ref.shape[0]
+        pick_ref[k * boxes : (k + 1) * boxes, :] = hit.astype(jnp.bfloat16)
+    for r, (far, near) in enumerate(sums_of(rows, far_within, slot_within, pick_ref, taken)):
+        sums_ref[0, r], sums_ref[1, r] = far, near
+
+
+def earlier_kernel(prev_ref, far_before, slot_before, pick_ref, sums_ref, out_ref, wide, rows, taken):
+    rays, boxes, _ = rows.shape
     rows_of_rays(prev_ref, wide, rows)
-    mix(rows, far_before, slot_before, mixed)
-    far, near = pick(pick_ref, mixed, far_cols // width * boxes)
-    far = (sums_ref[0] + far).astype(jnp.bfloat16).astype(jnp.float32)
-    near = (sums_ref[1] + near).astype(jnp.bfloat16).astype(jnp.float32)
-    both = far + near
-    for r in range(rays):
-        wide[pl.ds(r, boxes, stride=rays), :] = both[:, r * width : (r + 1) * width]
+    for r, (far, near) in enumerate(sums_of(rows, far_before, slot_before, pick_ref, taken)):
+        far = (sums_ref[0, r] + far).astype(jnp.bfloat16).astype(jnp.float32)
+        near = (sums_ref[1, r] + near).astype(jnp.bfloat16).astype(jnp.float32)
+        wide[pl.ds(r, boxes, stride=rays), :] = far + near
     run = wide.shape[0] // len(CHIPS)
     for n in range(0, len(CHIPS), 2):
         two = [wide[chip * run : (chip + 1) * run, :] for chip in CHIPS[n : n + 2]]
@@ -158,20 +151,20 @@
     size = lax.axis_size("tm")
     earlier = lax.ppermute(current, "tm", [(i, i + 1) for i in range(size - 1)])
 
-    far_before = jax.ShapeDtypeStruct((rays, width, offsets * width), jnp.bfloat16)
-    slot_before = jax.ShapeDtypeStruct((width, slots * width), jnp.bfloat16)
+    far_before = jax.ShapeDtypeStruct((rays, offsets * width, width), jnp.bfloat16)
+    slot_before = jax.ShapeDtypeStruct((slots * width, width), jnp.bfloat16)
     work = [
         pltpu.VMEM((devs * mid, width), jnp.float32),
         pltpu.VMEM((rays, boxes, width), jnp.bfloat16),
-        pltpu.VMEM(((offsets + slots) * boxes, rays * width), jnp.bfloat16),
+        pltpu.VMEM((rays, boxes, (offsets + slots) * width), jnp.bfloat16),
     ]
     begun = pl.pallas_call(
         current_kernel,
         out_shape=(
             far_before,
             slot_before,
-            jax.ShapeDtypeStruct((boxes, (offsets + slots) * boxes), jnp.bfloat16),
-            jax.ShapeDtypeStruct((2, boxes, rays * width), jnp.float32),
+            jax.ShapeDtypeStruct(((offsets + slots) * boxes, boxes), jnp.bfloat16),
+            jax.ShapeDtypeStruct((2, rays, boxes, width), jnp.float32),
         ),
         in_specs=[HBM] * 4 + [VMEM],
         out_specs=(VMEM,) * 4,

time: 52.8 us -> 52.9 us (level)
  transfers between devices with their start and end apart: 1 -> 1, of which waited for: 0 -> 0; matrix products, arithmetic and copies ran while one was open for 0% -> 0% of each run, Pallas kernels for 5% -> 6%
where the time goes in v4:
time: 52.9 us; the launch traced here: 52.5 us
  blocking collectives  43 us (81%)
  Pallas kernels  6.37 us (12%)
  starting transfers between devices  3.11 us (6%)
    all_to_all x2, blocking collectives, exchange(): lax.all_to_all(chunks, 'space', split_axis=0, concat_axis=0, axis_index_g...  43 us
    ppermute x1, starting transfers between devices, body(): earlier = lax.ppermute(current, 'tm', [(i, i + 1) for i in range(size - 1)])  3.11 us
    pallas_call x1, Pallas kernels, body(): pl.pallas_call(current_kernel, out_shape=(far_before, slot_before, jax.Sh...  3.03 us
    pallas_call x1, Pallas kernels, body(): pl.pallas_call(earlier_kernel, out_shape=jax.ShapeDtypeStruct((devs * mid...  1.59 us
  transfers between devices with their start and end apart: 1, of which 0 were waited for; matrix products, arithmetic and copies ran while one was open for 0% of the time, Pallas kernels for 6%

profile of v4, /device:TPU:1, one launch (start us, length us, event | category | flops | bytes accessed | tf_op | source)
XLA Modules:
  0.0 52.5 jit_solution(4879398432408387654)
XLA Ops:
  0.0 1.0 %parts.1 = bf16[128,2,2,128]{3,2,1,0:T(2,128)(2,1)S(1)} custom-call(bf16[2,128,2,128]{3,2,1,0:T(2,128)(2,1)} %bitcast.14), custom_call_target="tpu_custom_call" | custom-call | tf_op jit(solution)/shard_map/parts/pallas_call | solution.py:141
  1.0 25.4 %all_to_all.10 = bf16[128,4,128]{2,1,0:T(4,128)(2,1)S(1)} all-to-all(bf16[128,4,128]{2,1,0:T(4,128)(2,1)S(1)} %bitcast.11), channel_id=1, replica_groups={{72,73,8,9,104,105,40,41,88,89,24,25,120,121,56,57,64,65,0,1,96,97,32,3..., dimensions={0} | all-to-all | bytes 262144 | tf_op jit(solution)/shard_map/all_to_all | solution.py:23
  26.4 3.1 %collective-permute-start = (bf16[128,4,128]{2,1,0:T(4,128)(2,1)S(1)}, bf16[128,4,128]{2,1,0:T(4,128)(2,1)S(1)}, u32[]{:S(2)}, u32[]{:S(2)}) collective-permute-start(bf16[128,4,128]{2,1,0:T(4,128)(2,1)S(1)} %all_to_all.10), channel_id=1, source_target_pairs={{0,128},{128,256},{256,384},{1,129},{129,257},{257,385},{2,130},{1... | collective-permute-start | bytes 393224 | tf_op jit(solution)/shard_map/ppermute | solution.py:152
  29.6 3.0 %current.1 = (bf16[2,1536,128]{2,1,0:T(8,128)(2,1)S(1)}, bf16[1024,128]{1,0:T(8,128)(2,1)S(1)}, bf16[5120,256]{1,0:T(8,128)(2,1)S(1)}, f32[2,2,256,128]{3,2,1,0:T(8,128)S(1)}) custom-call(s32[12,256]{1,0:T(8,128)} %bitcast.15, s32[8,256]{1,0:T(8,128)} %bitcast.16, f32[12,2,128]{2,1,0:T(2,128)} %trans_hbm.1, f32[8,128]{1,0:T(8,128)} %slot_hbm.1, ...), custom_call_target="tpu_custom_call" | custom-call | flops 1000000000 | bytes 6000000 | tf_op jit(solution)/shard_map/current/pallas_call | solution.py:161
  32.6 0.0 collective-permute-done
  32.6 1.6 %earlier.1 = bf16[512,128]{1,0:T(8,128)(2,1)S(1)} custom-call(bf16[512,128]{1,0:T(8,128)(2,1)S(1)} %bitcast.12, bf16[2,1536,128]{2,1,0:T(8,128)(2,1)S(1)} %get-tuple-element.9.far_before, bf16[1024,128]{1,0:T(8,128)(2,1)S(1)} %get-tuple-element.10.slot_before, bf16[5120,256]{1,0:T(8,128)(2,1)S(1)} %get-tuple-element.11.pick_ref, ...), custom_call_target="tpu_custom_call" | custom-call | flops 1000000000 | bytes 6000000 | tf_op jit(solution)/shard_map/earlier/pallas_call | solution.py:191
  34.2 17.6 %all_to_all.11 = bf16[128,4,128]{2,1,0:T(4,128)(2,1)S(1)} all-to-all(bf16[128,4,128]{2,1,0:T(4,128)(2,1)S(1)} %bitcast.9), channel_id=1, replica_groups={{72,73,8,9,104,105,40,41,88,89,24,25,120,121,56,57,64,65,0,1,96,97,32,3..., dimensions={0} | all-to-all | bytes 262144 | tf_op jit(solution)/shard_map/all_to_all | solution.py:23
  51.8 0.8 %whole.1 = bf16[2,128,2,128]{3,2,1,0:T(2,128)(2,1)} custom-call(bf16[128,2,2,128]{3,2,1,0:T(2,128)(2,1)S(1)} %bitcast.10), custom_call_target="tpu_custom_call" | custom-call | tf_op jit(solution)/shard_map/whole/pallas_call | solution.py:202
Async XLA Ops:
  26.4 6.2 %collective-permute-start = (bf16[128,4,128]{2,1,0:T(4,128)(2,1)S(1)}, bf16[128,4,128]{2,1,0:T(4,128)(2,1)S(1)}, u32[]{:S(2)}, u32[]{:S(2)}) collective-permute-start(bf16[128,4,128]{2,1,0:T(4,128)(2,1)S(1)} %all_to_all.10), channel_id=1, source_target_pairs={{0,128},{128,256},{256,384},{1,129},{129,257},{257,385},{2,130},{1... | collective-permute-start | bytes 393224 | tf_op jit(solution)/shard_map/ppermute | solution.py:152

commit v5 on v4

--- a/solution.py
+++ b/solution.py
@@ -23,13 +23,22 @@
     return lax.all_to_all(chunks, "space", split_axis=0, concat_axis=0, axis_index_groups=[RANKS], tiled=True)
 
 
-def parts_kernel(signal_hbm, parts_ref, signal_ref, sem):
-    copy = pltpu.make_async_copy(signal_hbm, signal_ref, sem)
-    copy.start()
-    copy.wait()
-    for rank, dev in enumerate(RANKS):
-        for box in range(signal_ref.shape[0]):
-            parts_ref[rank, box] = signal_ref[box, dev]
+def pieces(array_ref):
+    boxes, devs = array_ref.shape[:2]
+    run = devs // 4
+    return [(box, range(first, first + run)) for box in range(boxes) for first in range(0, devs, run)]
+
+
+def parts_kernel(signal_hbm, parts_ref, signal_ref, sems):
+    copies = []
+    for n, (box, own) in enumerate(pieces(signal_ref)):
+        place = (box, pl.ds(own.start, len(own)))
+        copies.append(pltpu.make_async_copy(signal_hbm.at[place], signal_ref.at[place], sems.at[n]))
+        copies[-1].start()
+    for copy, (box, own) in zip(copies, pieces(signal_ref)):
+        copy.wait()
+        for dev in own:
+            parts_ref[RANKS.index(dev), box] = signal_ref[box, dev]
 
 
 def whole_kernel(parts_ref, field_hbm, field_ref, sem):
@@ -143,7 +152,7 @@
         out_shape=jax.ShapeDtypeStruct((devs, box_dev, rays, width), signal.dtype),
         in_specs=[HBM],
         out_specs=VMEM,
-        scratch_shapes=[pltpu.VMEM(split, signal.dtype), pltpu.SemaphoreType.DMA],
+        scratch_shapes=[pltpu.VMEM(split, signal.dtype), pltpu.SemaphoreType.DMA((4 * box_dev,))],
         compiler_params=pltpu.CompilerParams(vmem_limit_bytes=4 << 20),
         name="parts",
     )(in_hbm(signal.reshape(split)))

time: 52.9 us -> 53 us (level)
  no operation moved by 1% of the time
where the time goes in v5:
time: 53 us; the launch traced here: 52.4 us
  blocking collectives  43 us (81%)
  Pallas kernels  6.29 us (12%)
  starting transfers between devices  3.11 us (6%)
    all_to_all x2, blocking collectives, exchange(): lax.all_to_all(chunks, 'space', split_axis=0, concat_axis=0, axis_index_g...  43 us
    ppermute x1, starting transfers between devices, body(): earlier = lax.ppermute(current, 'tm', [(i, i + 1) for i in range(size - 1)])  3.11 us
    pallas_call x1, Pallas kernels, body(): pl.pallas_call(current_kernel, out_shape=(far_before, slot_before, jax.Sh...  3.03 us
    pallas_call x1, Pallas kernels, body(): pl.pallas_call(earlier_kernel, out_shape=jax.ShapeDtypeStruct((devs * mid...  1.59 us
  transfers between devices with their start and end apart: 1, of which 0 were waited for; matrix products, arithmetic and copies ran while one was open for 0% of the time, Pallas kernels for 6%

profile of v5, /device:TPU:1, one launch (start us, length us, event | category | flops | bytes accessed | tf_op | source)
XLA Modules:
  0.0 52.4 jit_solution(17647406727707066914)
XLA Ops:
  0.0 0.9 %parts.1 = bf16[128,2,2,128]{3,2,1,0:T(2,128)(2,1)S(1)} custom-call(bf16[2,128,2,128]{3,2,1,0:T(2,128)(2,1)} %bitcast.14), custom_call_target="tpu_custom_call" | custom-call | tf_op jit(solution)/shard_map/parts/pallas_call | solution.py:150
  0.9 25.4 %all_to_all.10 = bf16[128,4,128]{2,1,0:T(4,128)(2,1)S(1)} all-to-all(bf16[128,4,128]{2,1,0:T(4,128)(2,1)S(1)} %bitcast.11), channel_id=1, replica_groups={{72,73,8,9,104,105,40,41,88,89,24,25,120,121,56,57,64,65,0,1,96,97,32,3..., dimensions={0} | all-to-all | bytes 262144 | tf_op jit(solution)/shard_map/all_to_all | solution.py:23
  26.3 3.1 %collective-permute-start = (bf16[128,4,128]{2,1,0:T(4,128)(2,1)S(1)}, bf16[128,4,128]{2,1,0:T(4,128)(2,1)S(1)}, u32[]{:S(2)}, u32[]{:S(2)}) collective-permute-start(bf16[128,4,128]{2,1,0:T(4,128)(2,1)S(1)} %all_to_all.10), channel_id=1, source_target_pairs={{0,128},{128,256},{256,384},{1,129},{129,257},{257,385},{2,130},{1... | collective-permute-start | bytes 393224 | tf_op jit(solution)/shard_map/ppermute | solution.py:161
  29.5 3.0 %current.1 = (bf16[2,1536,128]{2,1,0:T(8,128)(2,1)S(1)}, bf16[1024,128]{1,0:T(8,128)(2,1)S(1)}, bf16[5120,256]{1,0:T(8,128)(2,1)S(1)}, f32[2,2,256,128]{3,2,1,0:T(8,128)S(1)}) custom-call(s32[12,256]{1,0:T(8,128)} %bitcast.15, s32[8,256]{1,0:T(8,128)} %bitcast.16, f32[12,2,128]{2,1,0:T(2,128)} %trans_hbm.1, f32[8,128]{1,0:T(8,128)} %slot_hbm.1, ...), custom_call_target="tpu_custom_call" | custom-call | flops 1000000000 | bytes 6000000 | tf_op jit(solution)/shard_map/current/pallas_call | solution.py:170
  32.5 0.0 collective-permute-done
  32.5 1.6 %earlier.1 = bf16[512,128]{1,0:T(8,128)(2,1)S(1)} custom-call(bf16[512,128]{1,0:T(8,128)(2,1)S(1)} %bitcast.12, bf16[2,1536,128]{2,1,0:T(8,128)(2,1)S(1)} %get-tuple-element.9.far_before, bf16[1024,128]{1,0:T(8,128)(2,1)S(1)} %get-tuple-element.10.slot_before, bf16[5120,256]{1,0:T(8,128)(2,1)S(1)} %get-tuple-element.11.pick_ref, ...), custom_call_target="tpu_custom_call" | custom-call | flops 1000000000 | bytes 6000000 | tf_op jit(solution)/shard_map/earlier/pallas_call | solution.py:200
  34.1 17.6 %all_to_all.11 = bf16[128,4,128]{2,1,0:T(4,128)(2,1)S(1)} all-to-all(bf16[128,4,128]{2,1,0:T(4,128)(2,1)S(1)} %bitcast.9), channel_id=1, replica_groups={{72,73,8,9,104,105,40,41,88,89,24,25,120,121,56,57,64,65,0,1,96,97,32,3..., dimensions={0} | all-to-all | bytes 262144 | tf_op jit(solution)/shard_map/all_to_all | solution.py:23
  51.7 0.8 %whole.1 = bf16[2,128,2,128]{3,2,1,0:T(2,128)(2,1)} custom-call(bf16[128,2,2,128]{3,2,1,0:T(2,128)(2,1)S(1)} %bitcast.10), custom_call_target="tpu_custom_call" | custom-call | tf_op jit(solution)/shard_map/whole/pallas_call | solution.py:211
Async XLA Ops:
  26.3 6.2 %collective-permute-start = (bf16[128,4,128]{2,1,0:T(4,128)(2,1)S(1)}, bf16[128,4,128]{2,1,0:T(4,128)(2,1)S(1)}, u32[]{:S(2)}, u32[]{:S(2)}) collective-permute-start(bf16[128,4,128]{2,1,0:T(4,128)(2,1)S(1)} %all_to_all.10), channel_id=1, source_target_pairs={{0,128},{128,256},{256,384},{1,129},{129,257},{257,385},{2,130},{1... | collective-permute-start | bytes 393224 | tf_op jit(solution)/shard_map/ppermute | solution.py:161
